TPU v7x, 32 devices: a whole 2x2x4 slice. The times are simulated.
32 devices in a mesh: row: 16 (over z, y, core), bundle: 2 (over x).
Axes of the slice: x: 2, y: 2, z: 4, core: 2. Of those that a mesh axis runs over, the one named last changes fastest.
Arguments:
- vectors: float32 [256, 32768], P('bundle', 'row'), may hold values from -6 to 6
- blocks: float32 [512, 64, 384], P('row'), may hold values from -0.30618622 to 0.30618622, as said below
- columns: int32 [512, 6], P('row'), may hold values from 0 to 511, as said below
- bounds: float32 [2], replicated, may hold values from -0.9 to 0.5, as said below
Outputs:
- basis: float32 [256, 32768], P(None, ('row', 'bundle'))
- factor: float32 [256, 256], replicated
Inputs may be any that keep to these rules, and one draw needn't show every extreme that they name: Slot 0 of block row i is i itself; every block column of block row i lies within 32 block rows of i, counted cyclically over the 512 block rows, and a distance of exactly 32 occurs; columns of one block row may repeat. `blocks`: together with columns they make H symmetric. bounds[0] < 0 < bounds[1].
All inputs are finite; a program needn't handle non-finite values.
Results may differ from a plain program's by a relative error of at most 0.00011.
Values sent between devices are 32-bit elements; how exact they have to be, the bound alone decides.
A program may use at most 64 MiB of HBM per device.

v0:
```python
import jax
import jax.numpy as jnp
from jax import lax
from jax.sharding import PartitionSpec as P


def extended_2(block, sides, width):
    for axis, dim in sides:
        count = lax.axis_size(axis)
        forward = [(i, i + 1) for i in range(count - 1)]
        forward.append((count - 1, 0))
        backward = [(target, source) for source, target in forward]
        low = lax.ppermute(
            lax.slice_in_dim(block, block.shape[dim] - width, None, axis=dim), axis, forward
        )
        high = lax.ppermute(lax.slice_in_dim(block, 0, width, axis=dim), axis, backward)
        block = jnp.concatenate([low, block, high], axis=dim)
    return block


def partner(value, axis, apart):
    mask = 2**apart
    pairs = [(source, source ^ mask) for source in range(lax.axis_size(axis))]
    return lax.ppermute(value, axis, pairs)


def local(vectors, blocks, columns, bounds):
    block_rows = blocks.shape[0]
    block_size = blocks.shape[1]
    slot_count = columns.shape[1]
    row_count = lax.axis_size("row")
    total_rows = block_rows * row_count
    first_row = lax.axis_index("row") * block_rows
    center = (bounds[0] + bounds[1]) * 0.5
    half = (bounds[1] - bounds[0]) * 0.5
    local_cols = jnp.mod(columns - first_row + block_rows, total_rows).reshape(-1)

    def apply_operator(field):
        extended = extended_2(field, (("row", 1),), block_rows * block_size)
        width = field.shape[0]
        extended3 = extended.reshape(width, 3 * block_rows, block_size)
        picked = jnp.take(extended3, local_cols, axis=1).reshape(
            width, block_rows, slot_count * block_size
        )
        result = jnp.einsum("iam,cim->cia", blocks, picked, precision=lax.Precision.HIGHEST)
        return result.reshape(width, block_rows * block_size)

    first = (apply_operator(vectors) - center * vectors) / half
    second = 2.0 * (apply_operator(first) - center * first) / half - vectors
    filtered = 2.0 * (apply_operator(second) - center * second) / half - first
    stacked = lax.all_to_all(filtered, "bundle", split_axis=1, concat_axis=0, tiled=True)
    gram = jnp.dot(
        stacked, stacked.T, precision=lax.Precision.HIGHEST, preferred_element_type=jnp.float32
    )
    for bit_index in range(row_count.bit_length() - 1):
        gram = gram + partner(gram, "row", bit_index)
    gram = lax.psum(gram, "bundle")
    lower = jnp.linalg.cholesky(gram)
    basis = jax.scipy.linalg.solve_triangular(lower, stacked, lower=True)
    return (basis, lower.T)


def solution(mesh):
    placed = (P("bundle", "row"), P("row", None, None), P("row", None), P())
    return jax.shard_map(
        local,
        mesh=mesh,
        in_specs=placed,
        out_specs=(P(None, ("row", "bundle")), P()),
        check_vma=False,
    )
```

profile of v0, /device:TPU:0, one launch (start us, length us, event | category | flops | bytes accessed | tf_op | source)
XLA Modules:
  0.0 289.9 jit_solution(4811276020961405723)
XLA Ops:
  7.2 2.7 copy.14
  10.4 5.0 %collective-permute-start.1 = (f32[128,2048]{0,1:T(8,128)}, f32[128,2048]{0,1:T(8,128)}, u32[]{:S(2)}, u32[]{:S(2)}) collective-permute-start(f32[128,2048]{0,1:T(8,128)} %copy.14), channel_id=1, source_target_pairs={{2,0},{4,2},{6,4},{8,6},{10,8},{12,10},{14,12},{16,14},{18,16},{20... | collective-permute-start | bytes 3145736 | tf_op jit(solution)/shard_map/ppermute | solution.py:16
  15.4 1.3 fusion.18
  20.0 8.2 %collective-permute-done = f32[128,2048]{0,1:T(8,128)} collective-permute-done((f32[128,2048]{0,1:T(8,128)}, f32[128,2048]{0,1:T(8,128)}, u32[]{:S(2)}, u32[]{:S(2)}) %collective-permute-start) | collective-permute-done | bytes 1048608 | tf_op jit(solution)/shard_map/ppermute | solution.py:13
  28.3 3.8 %pad_maximum_fusion = f32[128,6144]{0,1:T(8,128)} fusion(f32[128,2048]{0,1:T(8,128)} %collective-permute-done.1, f32[128,2048]{0,1:T(8,128)} %copy.14, f32[128,2048]{0,1:T(8,128)} %collective-permute-done), kind=kLoop, calls=%fused_computation.5 | loop fusion | flops 1572864 | bytes 6291456 | tf_op jit(solution)/shard_map/concatenate | solution.py:17
  32.0 5.5 %gather_fusion = f32[192,128,64]{1,2,0:T(8,128)} fusion(f32[128,96,64]{0,2,1:T(8,128)} %bitcast.93, s32[1024]{0:T(1024)S(1)} %pad_clamp_fusion), kind=kCustom, calls=%fused_computation.clone | custom fusion | bytes 12583680 | tf_op jit(solution)/shard_map/jit(_take)/gather | solution.py:42
  37.5 3.3 %broadcast_select_fusion.2 = f32[192,128,64]{1,2,0:T(8,128)S(1)} fusion(f32[192,128,64]{1,2,0:T(8,128)} %gather_fusion, pred[192]{0:T(512)(128)(4,1)S(1)} %compare_and_fusion), kind=kLoop, calls=%fused_computation.10 | loop fusion | flops 1572864 | bytes 12583104 | tf_op jit(solution)/shard_map/jit(_take)/select_n | solution.py:42
  40.8 4.8 %fusion.19 = f32[32,128,64]{1,2,0:T(8,128)S(1)} fusion(f32[128,32,384]{0,2,1:T(8,128)S(1)} %bitcast.96, f32[32,64,384]{2,1,0:T(8,128)S(1)} %copy-done), kind=kOutput, calls=%fused_computation.59 | convolution fusion | flops 1207959552 | bytes 10485760 | tf_op jit(solution)/shard_map/iam,cim->cia/dot_general | solution.py:45
  45.8 10.6 %collective-permute-start.2 = (f32[128,2048]{0,1:T(8,128)S(1)}, f32[128,2048]{0,1:T(8,128)S(1)}, u32[]{:S(2)}, u32[]{:S(2)}) collective-permute-start(f32[128,2048]{0,1:T(8,128)S(1)} %fusion.6), channel_id=1, source_target_pairs={{0,2},{2,4},{4,6},{6,8},{8,10},{10,12},{12,14},{14,16},{16,18},{18... | collective-permute-start | bytes 3145736 | tf_op jit(solution)/shard_map/ppermute | solution.py:13
  56.4 6.5 %collective-permute-done.2 = f32[128,2048]{0,1:T(8,128)S(1)} collective-permute-done((f32[128,2048]{0,1:T(8,128)S(1)}, f32[128,2048]{0,1:T(8,128)S(1)}, u32[]{:S(2)}, u32[]{:S(2)}) %collective-permute-start.2) | collective-permute-done | bytes 1048608 | tf_op jit(solution)/shard_map/ppermute | solution.py:13
  62.9 5.8 %collective-permute-done.3 = f32[128,2048]{0,1:T(8,128)S(1)} collective-permute-done((f32[128,2048]{0,1:T(8,128)S(1)}, f32[128,2048]{0,1:T(8,128)S(1)}, u32[]{:S(2)}, u32[]{:S(2)}) %collective-permute-start.3) | collective-permute-done | bytes 1048608 | tf_op jit(solution)/shard_map/ppermute | solution.py:16
  68.7 1.9 pad_maximum_fusion.1
  70.6 5.5 %gather_fusion.1 = f32[192,128,64]{1,2,0:T(8,128)} fusion(f32[128,96,64]{0,2,1:T(8,128)} %bitcast.94, s32[1024]{0:T(1024)S(1)} %pad_clamp_fusion), kind=kCustom, calls=%fused_computation.1.clone | custom fusion | bytes 12583680 | tf_op jit(solution)/shard_map/jit(_take)/gather | solution.py:42
  76.1 3.3 %broadcast_select_fusion.1 = f32[192,128,64]{1,2,0:T(8,128)S(1)} fusion(f32[192,128,64]{1,2,0:T(8,128)} %gather_fusion.1, pred[192]{0:T(512)(128)(4,1)S(1)} %compare_and_fusion), kind=kLoop, calls=%fused_computation.9 | loop fusion | flops 1572864 | bytes 12583104 | tf_op jit(solution)/shard_map/jit(_take)/select_n | solution.py:42
  79.4 4.8 %fusion.20 = f32[32,128,64]{1,2,0:T(8,128)S(1)} fusion(f32[128,32,384]{0,2,1:T(8,128)S(1)} %bitcast.97, f32[32,64,384]{2,1,0:T(8,128)S(1)} %copy-done), kind=kOutput, calls=%fused_computation.60 | convolution fusion | flops 1207959552 | bytes 10485760 | tf_op jit(solution)/shard_map/iam,cim->cia/dot_general | solution.py:45
  84.4 10.7 %collective-permute-start.4 = (f32[128,2048]{0,1:T(8,128)S(1)}, f32[128,2048]{0,1:T(8,128)S(1)}, u32[]{:S(2)}, u32[]{:S(2)}) collective-permute-start(f32[128,2048]{0,1:T(8,128)S(1)} %fusion.5), channel_id=1, source_target_pairs={{0,2},{2,4},{4,6},{6,8},{8,10},{10,12},{12,14},{14,16},{16,18},{18... | collective-permute-start | bytes 3145736 | tf_op jit(solution)/shard_map/ppermute | solution.py:13
  95.2 6.6 %collective-permute-done.4 = f32[128,2048]{0,1:T(8,128)S(1)} collective-permute-done((f32[128,2048]{0,1:T(8,128)S(1)}, f32[128,2048]{0,1:T(8,128)S(1)}, u32[]{:S(2)}, u32[]{:S(2)}) %collective-permute-start.4) | collective-permute-done | bytes 1048608 | tf_op jit(solution)/shard_map/ppermute | solution.py:13
  101.8 5.7 %collective-permute-done.5 = f32[128,2048]{0,1:T(8,128)S(1)} collective-permute-done((f32[128,2048]{0,1:T(8,128)S(1)}, f32[128,2048]{0,1:T(8,128)S(1)}, u32[]{:S(2)}, u32[]{:S(2)}) %collective-permute-start.5) | collective-permute-done | bytes 1048608 | tf_op jit(solution)/shard_map/ppermute | solution.py:16
  107.5 1.9 pad_maximum_fusion.2
  109.4 5.5 %gather_fusion.2 = f32[192,128,64]{1,2,0:T(8,128)} fusion(f32[128,96,64]{0,2,1:T(8,128)} %bitcast.92, s32[1024]{0:T(1024)S(1)} %pad_clamp_fusion), kind=kCustom, calls=%fused_computation.2.clone | custom fusion | bytes 12583680 | tf_op jit(solution)/shard_map/jit(_take)/gather | solution.py:42
  114.9 3.3 %broadcast_select_fusion = f32[192,128,64]{1,2,0:T(8,128)S(1)} fusion(f32[192,128,64]{1,2,0:T(8,128)} %gather_fusion.2, pred[192]{0:T(512)(128)(4,1)S(1)} %compare_and_fusion), kind=kLoop, calls=%fused_computation.8 | loop fusion | flops 1572864 | bytes 12583104 | tf_op jit(solution)/shard_map/jit(_take)/select_n | solution.py:42
  118.2 4.8 %fusion.21 = f32[32,128,64]{1,2,0:T(8,128)S(1)} fusion(f32[128,32,384]{0,2,1:T(8,128)S(1)} %bitcast.95, f32[32,64,384]{2,1,0:T(8,128)S(1)} %copy-done), kind=kOutput, calls=%fused_computation.61 | convolution fusion | flops 1207959552 | bytes 10485760 | tf_op jit(solution)/shard_map/iam,cim->cia/dot_general | solution.py:45
  123.0 1.1 fusion.2
  124.2 2.5 copy.22
  126.7 13.0 %all_to_all.19 = f32[128,2,1024]{2,0,1:T(8,128)S(1)} all-to-all(f32[128,2,1024]{2,0,1:T(8,128)} %copy.22), channel_id=1, replica_groups=mesh['row'=16,'bundle'=2] {'bundle'}, dimensions={1} | all-to-all | bytes 2097152 | tf_op jit(solution)/shard_map/all_to_all | solution.py:51
  141.7 11.3 %collective-permute-start.6 = (f32[256,256]{0,1:T(8,128)S(1)}, f32[256,256]{0,1:T(8,128)S(1)}, u32[]{:S(2)}, u32[]{:S(2)}) collective-permute-start(f32[256,256]{0,1:T(8,128)S(1)} %fusion.22), channel_id=1, source_target_pairs={{0,2},{2,0},{4,6},{6,4},{8,10},{10,8},{12,14},{14,12},{16,18},{18,... | collective-permute-start | bytes 786440 | tf_op jit(solution)/shard_map/ppermute | solution.py:24
  153.0 1.2 collective-permute-done.6
  154.2 3.9 %collective-permute-start.7 = (f32[256,256]{0,1:T(8,128)S(1)}, f32[256,256]{0,1:T(8,128)S(1)}, u32[]{:S(2)}, u32[]{:S(2)}) collective-permute-start(f32[256,256]{0,1:T(8,128)S(1)} %add.63), channel_id=1, source_target_pairs={{0,4},{2,6},{4,0},{6,2},{8,12},{10,14},{12,8},{14,10},{16,20},{18,... | collective-permute-start | bytes 786440 | tf_op jit(solution)/shard_map/ppermute | solution.py:24
  158.1 6.6 %collective-permute-done.7 = f32[256,256]{0,1:T(8,128)S(1)} collective-permute-done((f32[256,256]{0,1:T(8,128)S(1)}, f32[256,256]{0,1:T(8,128)S(1)}, u32[]{:S(2)}, u32[]{:S(2)}) %collective-permute-start.7) | collective-permute-done | bytes 262176 | tf_op jit(solution)/shard_map/ppermute | solution.py:24
  164.8 1.6 collective-permute-start.8
  166.4 6.3 %collective-permute-done.8 = f32[256,256]{0,1:T(8,128)S(1)} collective-permute-done((f32[256,256]{0,1:T(8,128)S(1)}, f32[256,256]{0,1:T(8,128)S(1)}, u32[]{:S(2)}, u32[]{:S(2)}) %collective-permute-start.8) | collective-permute-done | bytes 262176 | tf_op jit(solution)/shard_map/ppermute | solution.py:24
  172.7 2.7 collective-permute-start.9
  175.4 10.9 %collective-permute-done.9 = f32[256,256]{0,1:T(8,128)S(1)} collective-permute-done((f32[256,256]{0,1:T(8,128)S(1)}, f32[256,256]{0,1:T(8,128)S(1)}, u32[]{:S(2)}, u32[]{:S(2)}) %collective-permute-start.9) | collective-permute-done | bytes 262176 | tf_op jit(solution)/shard_map/ppermute | solution.py:24
  187.0 22.0 %all-reduce.3.cloned.1.call-done = f32[256,256]{0,1:T(8,128)} async-done(((f32[256,256]{0,1:T(8,128)}), f32[256,256]{0,1:T(8,128)}) %all-reduce.3.cloned.1.call-update) | async-done | bytes 262160 | tf_op jit(solution)/shard_map/psum | solution.py:57
  209.0 1.1 copy.25
  211.8 11.7 %cholesky.50 = f32[128,128]{1,0:T(8,128)S(1)} custom-call(f32[128,128]{1,0:T(8,128)S(1)} %cholesky.118), custom_call_target="Cholesky" | custom-call | tf_op jit(solution)/shard_map/jit(cholesky)/cholesky | solution.py:58
  223.5 9.8 %custom-call.15 = f32[1,128,128]{1,2,0:T(8,128)S(1)} custom-call(f32[1,128,128]{2,1,0:T(8,128)S(1)} %get-tuple-element.30), custom_call_target="InvertDiagBlocksLowerTriangular" | custom-call | tf_op jit(solution)/shard_map/jit(cholesky)/cholesky | solution.py:58
  233.3 1.0 constant_dynamic-update-slice_fusion.1
  234.4 1.1 convolution_subtract_fusion.1
  235.5 11.7 %cholesky.105 = f32[128,128]{1,0:T(8,128)S(1)} custom-call(f32[128,128]{1,0:T(8,128)S(1)} %convolution_subtract_fusion.1), custom_call_target="Cholesky" | custom-call | tf_op jit(solution)/shard_map/jit(cholesky)/cholesky | solution.py:58
  249.4 1.7 fusion.10
  251.1 5.5 %while.1 = (s32[]{:T(128)}, f32[256,256]{1,0:T(8,128)S(1)}, s32[2,2]{1,0:T(2,128)S(1)}, f32[2,128,128]{2,1,0:T(8,128)}, s32[]{:T(128)}) while((s32[]{:T(128)}, f32[256,256]{1,0:T(8,128)S(1)}, s32[2,2]{1,0:T(2,128)S(1)}, f32[2,128,128]{2,1,0:T(8,128)}, s32[]{:T(128)}) %tuple.32), condition=%wide.while_cond, body=%wide.while_body.sunk | while | flops 2 | bytes 132705 | solution.py:59
  251.8 2.1 bitcast_dynamic-update-slice_fusion.2
  254.6 2.1 bitcast_dynamic-update-slice_fusion.2
  256.7 20.5 %custom-call.16 = f32[2,128,128]{1,2,0:T(8,128)S(1)} custom-call(f32[2,128,128]{2,1,0:T(8,128)} %get-tuple-element.10), custom_call_target="InvertDiagBlocksLowerTriangular" | custom-call | tf_op jit(solution)/shard_map/jit(_solve_triangular)/triangular_solve | solution.py:59
  277.2 1.7 fusion.7
  278.8 1.6 convolution_subtract_fusion
  281.1 1.0 pad_maximum_fusion.3
  (58 shorter events, 10.0 us)
Async XLA Ops:
  7.2 33.7 %copy-start = (f32[32,64,384]{2,1,0:T(8,128)S(1)}, f32[32,64,384]{2,1,0:T(8,128)}, u32[]{:S(2)}) copy-start(f32[32,64,384]{2,1,0:T(8,128)} %param.7) | copy-start | bytes 9437188
  7.2 201.8 %all-reduce.3.cloned.1.call-start = ((), (), s32[]{:S(2)}) async-start(), calls=%async_computation.1 | async-start | bytes 524288 | tf_op jit(solution)/shard_map/psum | solution.py:57
  9.9 18.4 %collective-permute-start = (f32[128,2048]{0,1:T(8,128)}, f32[128,2048]{0,1:T(8,128)}, u32[]{:S(2)}, u32[]{:S(2)}) collective-permute-start(f32[128,2048]{0,1:T(8,128)} %copy.14), channel_id=1, source_target_pairs={{0,2},{2,4},{4,6},{6,8},{8,10},{10,12},{12,14},{14,16},{16,18},{18... | collective-permute-start | bytes 3145736 | tf_op jit(solution)/shard_map/ppermute | solution.py:13
  10.4 17.9 %collective-permute-start.1 = (f32[128,2048]{0,1:T(8,128)}, f32[128,2048]{0,1:T(8,128)}, u32[]{:S(2)}, u32[]{:S(2)}) collective-permute-start(f32[128,2048]{0,1:T(8,128)} %copy.14), channel_id=1, source_target_pairs={{2,0},{4,2},{6,4},{8,6},{10,8},{12,10},{14,12},{16,14},{18,16},{20... | collective-permute-start | bytes 3145736 | tf_op jit(solution)/shard_map/ppermute | solution.py:16
  40.8 4.8 %copy-start.5 = (f32[128,2048]{0,1:T(8,128)S(1)}, f32[128,2048]{0,1:T(8,128)}, u32[]{:S(2)}) copy-start(f32[128,2048]{0,1:T(8,128)} %copy.14) | copy-start | bytes 3145732
  45.8 24.8 %copy-start.2 = (f32[128,2048]{0,1:T(8,128)}, f32[128,2048]{0,1:T(8,128)S(1)}, u32[]{:S(2)}) copy-start(f32[128,2048]{0,1:T(8,128)S(1)} %fusion.6) | copy-start | bytes 3145732
  45.8 17.1 %collective-permute-start.2 = (f32[128,2048]{0,1:T(8,128)S(1)}, f32[128,2048]{0,1:T(8,128)S(1)}, u32[]{:S(2)}, u32[]{:S(2)}) collective-permute-start(f32[128,2048]{0,1:T(8,128)S(1)} %fusion.6), channel_id=1, source_target_pairs={{0,2},{2,4},{4,6},{6,8},{8,10},{10,12},{12,14},{14,16},{16,18},{18... | collective-permute-start | bytes 3145736 | tf_op jit(solution)/shard_map/ppermute | solution.py:13
  56.4 12.3 %collective-permute-start.3 = (f32[128,2048]{0,1:T(8,128)S(1)}, f32[128,2048]{0,1:T(8,128)S(1)}, u32[]{:S(2)}, u32[]{:S(2)}) collective-permute-start(f32[128,2048]{0,1:T(8,128)S(1)} %fusion.6), channel_id=1, source_target_pairs={{2,0},{4,2},{6,4},{8,6},{10,8},{12,10},{14,12},{16,14},{18,16},{20... | collective-permute-start | bytes 3145736 | tf_op jit(solution)/shard_map/ppermute | solution.py:16
  79.4 4.8 %copy-start.3 = (f32[128,2048]{0,1:T(8,128)S(1)}, f32[128,2048]{0,1:T(8,128)}, u32[]{:S(2)}) copy-start(f32[128,2048]{0,1:T(8,128)} %copy-done.2) | copy-start | bytes 3145732
  79.4 4.8 %copy-start.6 = (f32[128,2048]{0,1:T(8,128)S(1)}, f32[128,2048]{0,1:T(8,128)}, u32[]{:S(2)}) copy-start(f32[128,2048]{0,1:T(8,128)} %copy.14) | copy-start | bytes 3145732
  84.4 25.0 %copy-start.7 = (f32[128,2048]{0,1:T(8,128)}, f32[128,2048]{0,1:T(8,128)S(1)}, u32[]{:S(2)}) copy-start(f32[128,2048]{0,1:T(8,128)S(1)} %fusion.5) | copy-start | bytes 3145732
  84.4 17.3 %collective-permute-start.4 = (f32[128,2048]{0,1:T(8,128)S(1)}, f32[128,2048]{0,1:T(8,128)S(1)}, u32[]{:S(2)}, u32[]{:S(2)}) collective-permute-start(f32[128,2048]{0,1:T(8,128)S(1)} %fusion.5), channel_id=1, source_target_pairs={{0,2},{2,4},{4,6},{6,8},{8,10},{10,12},{12,14},{14,16},{16,18},{18... | collective-permute-start | bytes 3145736 | tf_op jit(solution)/shard_map/ppermute | solution.py:13
  95.2 12.3 %collective-permute-start.5 = (f32[128,2048]{0,1:T(8,128)S(1)}, f32[128,2048]{0,1:T(8,128)S(1)}, u32[]{:S(2)}, u32[]{:S(2)}) collective-permute-start(f32[128,2048]{0,1:T(8,128)S(1)} %fusion.5), channel_id=1, source_target_pairs={{2,0},{4,2},{6,4},{8,6},{10,8},{12,10},{14,12},{16,14},{18,16},{20... | collective-permute-start | bytes 3145736 | tf_op jit(solution)/shard_map/ppermute | solution.py:16
  118.2 4.8 %copy-start.4 = (f32[128,2048]{0,1:T(8,128)S(1)}, f32[128,2048]{0,1:T(8,128)}, u32[]{:S(2)}) copy-start(f32[128,2048]{0,1:T(8,128)} %copy-done.2) | copy-start | bytes 3145732
  118.2 4.8 %copy-start.8 = (f32[128,2048]{0,1:T(8,128)S(1)}, f32[128,2048]{0,1:T(8,128)}, u32[]{:S(2)}) copy-start(f32[128,2048]{0,1:T(8,128)} %copy-done.7) | copy-start | bytes 3145732
  139.7 1.0 copy-start.1
  141.7 12.5 %collective-permute-start.6 = (f32[256,256]{0,1:T(8,128)S(1)}, f32[256,256]{0,1:T(8,128)S(1)}, u32[]{:S(2)}, u32[]{:S(2)}) collective-permute-start(f32[256,256]{0,1:T(8,128)S(1)} %fusion.22), channel_id=1, source_target_pairs={{0,2},{2,0},{4,6},{6,4},{8,10},{10,8},{12,14},{14,12},{16,18},{18,... | collective-permute-start | bytes 786440 | tf_op jit(solution)/shard_map/ppermute | solution.py:24
  154.2 10.5 %collective-permute-start.7 = (f32[256,256]{0,1:T(8,128)S(1)}, f32[256,256]{0,1:T(8,128)S(1)}, u32[]{:S(2)}, u32[]{:S(2)}) collective-permute-start(f32[256,256]{0,1:T(8,128)S(1)} %add.63), channel_id=1, source_target_pairs={{0,4},{2,6},{4,0},{6,2},{8,12},{10,14},{12,8},{14,10},{16,20},{18,... | collective-permute-start | bytes 786440 | tf_op jit(solution)/shard_map/ppermute | solution.py:24
  164.8 7.9 %collective-permute-start.8 = (f32[256,256]{0,1:T(8,128)S(1)}, f32[256,256]{0,1:T(8,128)S(1)}, u32[]{:S(2)}, u32[]{:S(2)}) collective-permute-start(f32[256,256]{0,1:T(8,128)S(1)} %add.64), channel_id=1, source_target_pairs={{0,8},{2,10},{4,12},{6,14},{8,0},{10,2},{12,4},{14,6},{16,24},{18,... | collective-permute-start | bytes 786440 | tf_op jit(solution)/shard_map/ppermute | solution.py:24
  172.7 13.5 %collective-permute-start.9 = (f32[256,256]{0,1:T(8,128)S(1)}, f32[256,256]{0,1:T(8,128)S(1)}, u32[]{:S(2)}, u32[]{:S(2)}) collective-permute-start(f32[256,256]{0,1:T(8,128)S(1)} %add.65), channel_id=1, source_target_pairs={{0,16},{2,18},{4,20},{6,22},{8,24},{10,26},{12,28},{14,30},{16,0},... | collective-permute-start | bytes 786440 | tf_op jit(solution)/shard_map/ppermute | solution.py:24
  211.0 0.7 copy-start.11
  247.3 2.1 copy-start.9
  280.5 1.7 copy-start.10
Sparse Core Ops, SparseCore 0:
  187.1 21.8 all-reduce.2
where the time goes:
time: 291 us; the launch traced here: 290 us
  waiting for transfers between devices  79.7 us (27%)
  other arithmetic  78.6 us (27%)
  starting transfers between devices  46.3 us (16%)
  local copies, waits for them, and re-layouts  32.5 us (11%)
  matrix products  21.5 us (7%)
  between operations  18.2 us (6%)
  blocking collectives  13 us (4%)
    another operation x6, other arithmetic, local(): lower = jnp.linalg.cholesky(gram)  34 us
    ppermute x4, waiting for transfers between devices, partner(): return lax.ppermute(value, axis, pairs)  24.9 us
    psum x1, waiting for transfers between devices, local(): gram = lax.psum(gram, 'bundle')  22 us
    ppermute x3, starting transfers between devices, extended_2(): lax.ppermute(lax.slice_in_dim(block, block.shape[dim] - width, None, axis...  21.7 us
    another operation x3, other arithmetic, local(): basis = jax.scipy.linalg.solve_triangular(lower, stacked, lower=True)  21.5 us
    ppermute x3, waiting for transfers between devices, extended_2(): lax.ppermute(lax.slice_in_dim(block, block.shape[dim] - width, None, axis...  21.4 us
    ppermute x4, starting transfers between devices, partner(): return lax.ppermute(value, axis, pairs)  19.5 us
    gather x3, local copies, waits for them, and re-layouts, apply_operator(): jnp.take(extended3, local_cols, axis=1)  16.5 us
  transfers between devices with their start and end apart: 11, of which 10 were waited for; matrix products, arithmetic and copies ran while one was open for 1% of the time, Pallas kernels for 0%

commit v1 on v0

v1 whole, which is shorter than its diff:
```python
import functools

import jax
import jax.numpy as jnp
from jax import lax
from jax.experimental import pallas as pl
from jax.experimental.pallas import tpu as pltpu
from jax.sharding import PartitionSpec as P

MESH = pl.DeviceIdType.MESH
F32 = jnp.float32
BF16 = jnp.bfloat16
HIGHEST = lax.Precision.HIGHEST
VMEM_LIMIT = 56 * 1024 * 1024
PANEL = 64


def split(value):
    high = value.astype(BF16)
    return high, (value - high.astype(F32)).astype(BF16)


def filter_kernel(
    rows, bundles, cols_ref, bounds_ref, vec_ref, blocks_ref, stacked_ref, gram_ref,
    ablk, high, low, fields, halo, gram_in, halo_send, halo_recv, all_send, all_recv,
    gram_send, gram_recv,
):
    me = lax.axis_index("row")
    mine = lax.axis_index("bundle")
    br, bs = blocks_ref.shape[0], blocks_ref.shape[1]
    slots = cols_ref.shape[1]
    width = vec_ref.shape[0]
    total = br * rows
    right = lax.rem(me + 1, rows)
    left = lax.rem(me + rows - 1, rows)
    chunks = 4
    per = br // chunks

    row_bits = rows.bit_length() - 1
    bundle_bits = bundles.bit_length() - 1
    partners = []
    for bit in range(row_bits):
        mask = 1 << bit
        upper = lax.rem(lax.div(me, mask), 2)
        partners.append({"row": me + mask - 2 * mask * upper})
    for bit in range(bundle_bits):
        mask = 1 << bit
        upper = lax.rem(lax.div(mine, mask), 2)
        partners.append({"bundle": mine + mask - 2 * mask * upper})
    others = [{"bundle": lax.rem(mine + step, bundles)} for step in range(1, bundles)]

    barrier = pltpu.get_barrier_semaphore()
    greeted = [{"row": left}, {"row": right}] + partners + others
    for device in greeted:
        pl.semaphore_signal(barrier, inc=1, device_id=device, device_id_type=MESH)

    center = (bounds_ref[0] + bounds_ref[1]) * 0.5
    inverse = 1.0 / ((bounds_ref[1] - bounds_ref[0]) * 0.5)

    def halo_copies(step, chunk):
        part = pl.ds(chunk * per, per)
        return [
            pltpu.make_async_remote_copy(
                src_ref=fields.at[step, part],
                dst_ref=halo.at[step, side, part],
                send_sem=halo_send.at[step, side, chunk],
                recv_sem=halo_recv.at[step, side, chunk],
                device_id={"row": target},
                device_id_type=MESH,
            )
            for side, target in ((0, right), (1, left))
        ]

    def keep(slot, first, value):
        h, l = split(value)
        high[slot, pl.ds(first, value.shape[0])] = h
        low[slot, pl.ds(first, value.shape[0])] = l

    for chunk in range(chunks):
        span = per * bs
        piece = vec_ref[:, chunk * span:(chunk + 1) * span]
        turned = piece.T.reshape(per, bs, width)
        fields[0, chunk * per:(chunk + 1) * per] = turned
        if chunk == 0:
            pl.semaphore_wait(barrier, len(greeted))
        for copy in halo_copies(0, chunk):
            copy.start()
        keep(0, br + chunk * per, turned)

    @pl.loop(0, br)
    def _(i):
        h, l = split(blocks_ref[i])
        ablk[i, :bs] = h
        ablk[i, bs:] = l

    for step in range(3):
        slot, later = step % 2, (step + 1) % 2

        @pl.loop(0, chunks)
        def _(chunk):
            for side, copy in enumerate(halo_copies(step, chunk)):
                copy.wait_recv()
                keep(slot, side * 2 * br + chunk * per, halo[step, side, pl.ds(chunk * per, per)])

        @pl.loop(0, chunks)
        def _(chunk):
            @pl.loop(0, per, unroll=2)
            def _(inner):
                i = chunk * per + inner
                found_high, found_low = [], []
                for s in range(slots):
                    c = lax.rem(cols_ref[i, s] - me * br + br + total, total)
                    c = jnp.clip(c, 0, 3 * br - 1)
                    found_high.append(high[slot, c])
                    found_low.append(low[slot, c])
                b_high = jnp.concatenate(found_high, axis=0)
                b_low = jnp.concatenate(found_low, axis=0)
                a = ablk[i]
                if width % 128 == 0:
                    out = jnp.dot(
                        a, jnp.concatenate([b_high, b_low], axis=1), preferred_element_type=F32
                    )
                    p, q = out[:, :width], out[:, width:]
                    result = p[:bs] + (p[bs:] + q[:bs])
                else:
                    p = jnp.dot(a, b_high, preferred_element_type=F32)
                    q = jnp.dot(a[:bs], b_low, preferred_element_type=F32)
                    result = p[:bs] + (p[bs:] + q)
                value = (result - center * fields[step, i]) * inverse
                if step > 0:
                    value = 2.0 * value - fields[step - 1, i]
                fields[step + 1, i] = value
                if step < 2:
                    h, l = split(value)
                    high[later, br + i] = h
                    low[later, br + i] = l

            if step < 2:
                for copy in halo_copies(step + 1, chunk):
                    copy.start()

    share = br // bundles

    def stack_copy(index):
        target = others[index]
        return pltpu.make_async_remote_copy(
            src_ref=fields.at[3, pl.ds(target["bundle"] * share, share)],
            dst_ref=stacked_ref.at[mine],
            send_sem=all_send.at[index],
            recv_sem=all_recv.at[index],
            device_id=target,
            device_id_type=MESH,
        )

    for index in range(bundles - 1):
        stack_copy(index).start()
    stacked_ref[mine] = fields[3, pl.ds(mine * share, share)]
    for index in range(bundles - 1):
        stack_copy(index).wait_recv()

    held = [stacked_ref[b].reshape(share * bs, width) for b in range(bundles)]
    whole = jnp.concatenate(held, axis=1)
    h, l = split(whole)
    over_rows = (((0,), (0,)), ((), ()))
    main = lax.dot_general(h, h, over_rows, preferred_element_type=F32)
    cross = lax.dot_general(h, l, over_rows, preferred_element_type=F32)
    gram_in[0] = main + (cross + cross.T)

    for index, device in enumerate(partners):
        copy = pltpu.make_async_remote_copy(
            src_ref=gram_in.at[2 * index],
            dst_ref=gram_in.at[2 * index + 1],
            send_sem=gram_send.at[index],
            recv_sem=gram_recv.at[index],
            device_id=device,
            device_id_type=MESH,
        )
        copy.start()
        copy.wait_recv()
        gram_in[2 * index + 2] = gram_in[2 * index] + gram_in[2 * index + 1]
        copy.wait_send()
    gram_ref[...] = gram_in[2 * len(partners)]

    for index in range(bundles - 1):
        stack_copy(index).wait_send()

    for step in range(3):
        @pl.loop(0, chunks)
        def _(chunk):
            for copy in halo_copies(step, chunk):
                copy.wait_send()


def triangular_inverse(block):
    size = block.shape[0]
    row = lax.broadcasted_iota(jnp.int32, (size, size), 0)
    col = lax.broadcasted_iota(jnp.int32, (size, size), 1)
    eye = (row == col).astype(F32)
    work = jnp.concatenate([block, eye], axis=1)
    index = lax.broadcasted_iota(jnp.int32, (size, 1), 0)
    scales = jnp.zeros((size, 1), F32)
    for k in range(size):
        pivot = work[k:k + 1, k:k + 1]
        line = work[k:k + 1, :] * (1.0 / pivot)
        factor = jnp.where(index > k, work[:, k:k + 1], 0.0)
        scales = jnp.where(index == k, pivot, scales)
        work = work - factor * line
    return work[:, size:] * lax.rsqrt(scales)


def factor_kernel(gram_ref, stacked_ref, basis_ref, factor_ref, work):
    n = gram_ref.shape[0]
    row = lax.broadcasted_iota(jnp.int32, (n, n), 0)
    col = lax.broadcasted_iota(jnp.int32, (n, n), 1)
    work[:, :n] = gram_ref[...]
    work[:, n:] = (row == col).astype(F32)
    for first in range(0, n, PANEL):
        last = first + PANEL
        inverse = triangular_inverse(work[first:last, first:last])
        lines = jnp.dot(inverse, work[first:last, :], precision=HIGHEST, preferred_element_type=F32)
        work[first:last, :] = lines
        if last < n:
            work[last:, :] = work[last:, :] - lax.dot_general(
                lines[:, last:n], lines, (((0,), (0,)), ((), ())),
                precision=HIGHEST, preferred_element_type=F32,
            )
    factor_ref[...] = jnp.where(col >= row, work[:, :n], 0.0)
    solver = jnp.where(col <= row, work[:, n:], 0.0)
    bundles, share, bs, width = stacked_ref.shape
    h, l = split(solver)
    over_last = (((1,), (1,)), ((), ()))
    held = [stacked_ref[b].reshape(share * bs, width) for b in range(bundles)]
    fh, fl = split(jnp.concatenate(held, axis=1))
    dot = lambda a, b: lax.dot_general(a, b, over_last, preferred_element_type=F32)
    basis_ref[...] = dot(h, fh) + (dot(h, fl) + dot(l, fh))


def solution(mesh):
    rows, bundles = mesh.shape["row"], mesh.shape["bundle"]
    steps = (rows.bit_length() - 1) + (bundles.bit_length() - 1)
    vmem = pl.BlockSpec(memory_space=pltpu.VMEM)
    smem = pl.BlockSpec(memory_space=pltpu.SMEM)

    def local(vectors, blocks, columns, bounds):
        br, bs, wide = blocks.shape
        width = vectors.shape[0]
        count = width * bundles
        share = br // bundles
        stacked, gram = pl.pallas_call(
            functools.partial(filter_kernel, rows, bundles),
            out_shape=(
                jax.ShapeDtypeStruct((bundles, share, bs, width), F32),
                jax.ShapeDtypeStruct((count, count), F32),
            ),
            in_specs=[smem, smem, vmem, vmem],
            out_specs=(vmem, vmem),
            scratch_shapes=[
                pltpu.VMEM((br, 2 * bs, wide), BF16),
                pltpu.VMEM((2, 3 * br, bs, width), BF16),
                pltpu.VMEM((2, 3 * br, bs, width), BF16),
                pltpu.VMEM((4, br, bs, width), F32),
                pltpu.VMEM((3, 2, br, bs, width), F32),
                pltpu.VMEM((2 * steps + 1, count, count), F32),
                pltpu.SemaphoreType.DMA((3, 2, 4)),
                pltpu.SemaphoreType.DMA((3, 2, 4)),
                pltpu.SemaphoreType.DMA((max(bundles - 1, 1),)),
                pltpu.SemaphoreType.DMA((max(bundles - 1, 1),)),
                pltpu.SemaphoreType.DMA((steps,)),
                pltpu.SemaphoreType.DMA((steps,)),
            ],
            compiler_params=pltpu.CompilerParams(
                collective_id=0, has_side_effects=True, vmem_limit_bytes=VMEM_LIMIT
            ),
        )(columns, bounds, vectors, blocks)
        return pl.pallas_call(
            factor_kernel,
            out_shape=(
                jax.ShapeDtypeStruct((count, share * bs), F32),
                jax.ShapeDtypeStruct((count, count), F32),
            ),
            in_specs=[vmem, vmem],
            out_specs=(vmem, vmem),
            scratch_shapes=[pltpu.VMEM((count, 2 * count), F32)],
            compiler_params=pltpu.CompilerParams(vmem_limit_bytes=VMEM_LIMIT),
        )(gram, stacked)

    placed = (P("bundle", "row"), P("row", None, None), P("row", None), P())
    return jax.shard_map(
        local,
        mesh=mesh,
        in_specs=placed,
        out_specs=(P(None, ("row", "bundle")), P()),
        check_vma=False,
    )
```

time: 291 us -> 166 us (0.57)
  Pallas kernels: 0 us -> 164 us
  waiting for transfers between devices: 79.7 us -> 0 us
  other arithmetic: 78.6 us -> 0 us
  starting transfers between devices: 46.3 us -> 0 us
  local copies, waits for them, and re-layouts: 32.5 us -> 1.37 us
  matrix products: 21.5 us -> 0 us
  between operations: 18.2 us -> 0.64 us
  blocking collectives: 13 us -> 0 us
    pallas_call x0 -> x2, Pallas kernels: none -> 164 us  [the longest x1 135 us: local(): pl.pallas_call(functools.partial(filter_kernel, rows, bundles), out_shape...]
    ppermute x10 -> x0, waiting for transfers between devices: 57.8 us -> none  [the longest x4 24.9 us: partner(): return lax.ppermute(value, axis, pairs)]
    another operation x9 -> x0, other arithmetic: 55.5 us -> none  [the longest x6 34 us: local(): lower = jnp.linalg.cholesky(gram)]
    ppermute x10 -> x0, starting transfers between devices: 46.3 us -> none  [the longest x3 21.7 us: extended_2(): lax.ppermute(lax.slice_in_dim(block, block.shape[dim] - width, None, axis...]
    psum x1 -> x0, waiting for transfers between devices: 22 us -> none  [local(): gram = lax.psum(gram, 'bundle')]
    gather x3 -> x0, local copies, waits for them, and re-layouts: 16.5 us -> none  [apply_operator(): jnp.take(extended3, local_cols, axis=1)]
    dot_general x4 -> x0, matrix products: 15.5 us -> none  [the longest x3 14.4 us: apply_operator(): jnp.einsum('iam,cim->cia', blocks, picked, precision=lax.Precision.HIGHEST)]
    all_to_all x1 -> x0, blocking collectives: 13 us -> none  [local(): lax.all_to_all(filtered, 'bundle', split_axis=1, concat_axis=0, tiled=True)]
  transfers between devices with their start and end apart: 11 -> 0, of which waited for: 10 -> 0; matrix products, arithmetic and copies ran while one was open for 1% -> 0% of each run, Pallas kernels for 0% -> 0%
where the time goes in v1:
time: 166 us
  Pallas kernels  164 us (99%)
    pallas_call x1, Pallas kernels, local(): pl.pallas_call(functools.partial(filter_kernel, rows, bundles), out_shape...  135 us
    pallas_call x1, Pallas kernels, local(): pl.pallas_call(factor_kernel, out_shape=(jax.ShapeDtypeStruct((count, sha...  28.4 us

profile of v1, /device:TPU:0, one launch (start us, length us, event | category | flops | bytes accessed | tf_op | source)
XLA Modules:
  0.0 165.8 jit_solution(11375707909673778001)
XLA Ops:
  0.6 1.4 copy.6.cols_ref
  2.0 135.4 %shard_map.59 = (f32[2,16,64,128]{3,2,1,0:T(8,128)}, f32[256,256]{1,0:T(8,128)}) custom-call(s32[32,6]{1,0:T(8,128)} %copy.6.cols_ref, f32[2]{0:T(128)} %bounds_ref.1, f32[128,2048]{1,0:T(8,128)} %vec_ref.1, f32[32,64,384]{2,1,0:T(8,128)} %blocks_ref.1), custom_call_target="tpu_custom_call" | custom-call | tf_op jit(solution)/shard_map/pallas_call | solution.py:249
  137.4 28.4 %shard_map.60 = (f32[256,1024]{1,0:T(8,128)}, f32[256,256]{1,0:T(8,128)}) custom-call(f32[256,256]{1,0:T(8,128)} %get-tuple-element.4.gram_ref, f32[2,16,64,128]{3,2,1,0:T(8,128)} %get-tuple-element.5.stacked_ref), custom_call_target="tpu_custom_call" | custom-call | tf_op jit(solution)/shard_map/pallas_call | solution.py:275

commit v2 on v1

v2 whole, which is shorter than its diff:
```python
import functools

import jax
import jax.numpy as jnp
from jax import lax
from jax.experimental import pallas as pl
from jax.experimental.pallas import tpu as pltpu
from jax.sharding import PartitionSpec as P

MESH = pl.DeviceIdType.MESH
F32 = jnp.float32
BF16 = jnp.bfloat16
HIGHEST = lax.Precision.HIGHEST
VMEM_LIMIT = 56 * 1024 * 1024
PANEL = 64
GROUP = 4
OVER_ROWS = (((0,), (0,)), ((), ()))
OVER_LAST = (((1,), (1,)), ((), ()))


def split(value):
    high = value.astype(BF16)
    return high, (value - high.astype(F32)).astype(BF16)


def filter_kernel(
    rows, bundles, out_count, cols_ref, bounds_ref, vec_ref, blocks_ref, *refs,
):
    outs = refs[:out_count]
    (
        ablk, high, low, fields, halo, sums, lines, halo_send, halo_recv, all_send, all_recv,
        sum_send, sum_recv,
    ) = refs[out_count:]
    me = lax.axis_index("row")
    mine = lax.axis_index("bundle")
    br, bs = blocks_ref.shape[0], blocks_ref.shape[1]
    slots = cols_ref.shape[1]
    width = vec_ref.shape[0]
    total = br * rows
    right = lax.rem(me + 1, rows)
    left = lax.rem(me + rows - 1, rows)
    chunks = 4
    per = br // chunks

    row_bits = rows.bit_length() - 1
    bundle_bits = bundles.bit_length() - 1
    partners = []
    for bit in range(row_bits):
        mask = 1 << bit
        upper = lax.rem(lax.div(me, mask), 2)
        partners.append({"row": me + mask - 2 * mask * upper})
    for bit in range(bundle_bits):
        mask = 1 << bit
        upper = lax.rem(lax.div(mine, mask), 2)
        partners.append({"bundle": mine + mask - 2 * mask * upper})
    others = [{"bundle": lax.rem(mine + step, bundles)} for step in range(1, bundles)]

    barrier = pltpu.get_barrier_semaphore()
    greeted = [{"row": left}, {"row": right}] + partners + others
    for device in greeted:
        pl.semaphore_signal(barrier, inc=1, device_id=device, device_id_type=MESH)

    center = (bounds_ref[0] + bounds_ref[1]) * 0.5
    inverse = 1.0 / ((bounds_ref[1] - bounds_ref[0]) * 0.5)

    def halo_copies(step, chunk):
        part = pl.ds(chunk * per, per)
        return [
            pltpu.make_async_remote_copy(
                src_ref=fields.at[step, part],
                dst_ref=halo.at[step, side, part],
                send_sem=halo_send.at[step, side, chunk],
                recv_sem=halo_recv.at[step, side, chunk],
                device_id={"row": target},
                device_id_type=MESH,
            )
            for side, target in ((0, right), (1, left))
        ]

    def keep(slot, first, value):
        h, l = split(value)
        high[slot, pl.ds(first, value.shape[0])] = h
        low[slot, pl.ds(first, value.shape[0])] = l

    for chunk in range(chunks):
        span = per * bs
        piece = vec_ref[:, chunk * span:(chunk + 1) * span]
        turned = piece.T.reshape(per, bs, width)
        fields[0, chunk * per:(chunk + 1) * per] = turned
        if chunk == 0:
            pl.semaphore_wait(barrier, len(greeted))
        for copy in halo_copies(0, chunk):
            copy.start()
        keep(0, br + chunk * per, turned)

    @pl.loop(0, br)
    def _(i):
        h, l = split(blocks_ref[i])
        ablk[i, :bs] = h
        ablk[i, bs:] = l

    def receive(step):
        slot = step % 2

        @pl.loop(0, chunks)
        def _(chunk):
            for side, copy in enumerate(halo_copies(step, chunk)):
                copy.wait_recv()
                keep(slot, side * 2 * br + chunk * per, halo[step, side, pl.ds(chunk * per, per)])

    def apply_chunk(step, chunk):
        slot, later = step % 2, (step + 1) % 2

        @pl.loop(0, per, unroll=2)
        def _(inner):
            i = chunk * per + inner
            found_high, found_low = [], []
            for s in range(slots):
                c = lax.rem(cols_ref[i, s] - me * br + br + total, total)
                c = jnp.clip(c, 0, 3 * br - 1)
                found_high.append(high[slot, c])
                found_low.append(low[slot, c])
            b_high = jnp.concatenate(found_high, axis=0)
            b_low = jnp.concatenate(found_low, axis=0)
            a = ablk[i]
            if width % 128 == 0:
                out = jnp.dot(
                    a, jnp.concatenate([b_high, b_low], axis=1), preferred_element_type=F32
                )
                p, q = out[:, :width], out[:, width:]
                result = p[:bs] + (p[bs:] + q[:bs])
            else:
                p = jnp.dot(a, b_high, preferred_element_type=F32)
                q = jnp.dot(a[:bs], b_low, preferred_element_type=F32)
                result = p[:bs] + (p[bs:] + q)
            value = (result - center * fields[step, i]) * inverse
            if step > 0:
                value = 2.0 * value - fields[step - 1, i]
            fields[step + 1, i] = value
            if step < 2:
                h, l = split(value)
                high[later, br + i] = h
                low[later, br + i] = l

    for step in range(2):
        receive(step)

        @pl.loop(0, chunks)
        def _(chunk):
            apply_chunk(step, chunk)
            for copy in halo_copies(step + 1, chunk):
                copy.start()

    share = br // bundles
    receive(2)

    def sum_copy(index, device):
        return pltpu.make_async_remote_copy(
            src_ref=sums.at[2 * index],
            dst_ref=sums.at[2 * index + 1],
            send_sem=sum_send.at[index],
            recv_sem=sum_recv.at[index],
            device_id=device,
            device_id_type=MESH,
        )

    def sum_step(index, device, beside=None):
        copy = sum_copy(index, device)
        copy.start()
        if beside is not None:
            next(beside, None)
        copy.wait()
        sums[2 * index + 2] = sums[2 * index] + sums[2 * index + 1]

    if is_paired(bundles, width):
        stacked_ref, corner_ref, diag_ref, cross_ref = outs
        theirs = 1 - mine
        half = chunks // 2

        def stack_copy(part):
            rows_of = pl.ds(theirs * share + part * per, per)
            return pltpu.make_async_remote_copy(
                src_ref=fields.at[3, rows_of],
                dst_ref=stacked_ref.at[mine, pl.ds(part * per, per)],
                send_sem=all_send.at[part],
                recv_sem=all_recv.at[part],
                device_id={"bundle": theirs},
                device_id_type=MESH,
            )

        @pl.loop(0, half)
        def _(part):
            apply_chunk(2, theirs * half + part)
            stack_copy(part).start()

        @pl.loop(0, half)
        def _(part):
            apply_chunk(2, mine * half + part)

        stacked_ref[mine] = fields[3, pl.ds(mine * share, share)]
        h, l = split(fields[3].reshape(br * bs, width))
        both = lax.dot_general(
            h, jnp.concatenate([h, l], axis=1), OVER_ROWS, preferred_element_type=F32
        )
        sums[0] = both[:, :width] + (both[:, width:] + both[:, width:].T)
        for index in range(row_bits):
            sum_step(index, partners[index])
        done = 2 * row_bits
        diag_ref[mine] = sums[done]
        diag_copy = pltpu.make_async_remote_copy(
            src_ref=sums.at[done],
            dst_ref=diag_ref.at[mine],
            send_sem=all_send.at[half],
            recv_sem=all_recv.at[half],
            device_id={"bundle": theirs},
            device_id_type=MESH,
        )
        diag_copy.start()
        for part in range(half):
            stack_copy(part).wait_recv()
        h0, l0 = split(stacked_ref[0].reshape(share * bs, width))
        h1, l1 = split(stacked_ref[1].reshape(share * bs, width))
        both = lax.dot_general(
            h0, jnp.concatenate([h1, l1], axis=1), OVER_ROWS, preferred_element_type=F32
        )
        rest = lax.dot_general(l0, h1, OVER_ROWS, preferred_element_type=F32)
        sums[done + 2] = both[:, :width] + (both[:, width:] + rest)
        diag_copy.wait()
        found = []
        pieces = factor_steps(diag_ref[0], lines, found)
        for bit, device in enumerate(partners):
            sum_step(row_bits + 1 + bit, device, pieces)
        for _ in pieces:
            pass
        cross_ref[...] = sums[done + 2 + 2 * len(partners)]
        corner_ref[0], corner_ref[1] = found
        for part in range(half):
            stack_copy(part).wait_send()
    else:
        stacked_ref, gram_ref = outs

        @pl.loop(0, chunks)
        def _(chunk):
            apply_chunk(2, chunk)

        def stack_copy(index):
            target = others[index]
            return pltpu.make_async_remote_copy(
                src_ref=fields.at[3, pl.ds(target["bundle"] * share, share)],
                dst_ref=stacked_ref.at[mine],
                send_sem=all_send.at[index],
                recv_sem=all_recv.at[index],
                device_id=target,
                device_id_type=MESH,
            )

        for index in range(bundles - 1):
            stack_copy(index).start()
        stacked_ref[mine] = fields[3, pl.ds(mine * share, share)]
        for index in range(bundles - 1):
            stack_copy(index).wait_recv()
        held = [stacked_ref[b].reshape(share * bs, width) for b in range(bundles)]
        h, l = split(jnp.concatenate(held, axis=1))
        main = lax.dot_general(h, h, OVER_ROWS, preferred_element_type=F32)
        cross = lax.dot_general(h, l, OVER_ROWS, preferred_element_type=F32)
        sums[0] = main + (cross + cross.T)
        for index, device in enumerate(partners):
            sum_step(index, device)
        gram_ref[...] = sums[2 * len(partners)]
        for index in range(bundles - 1):
            stack_copy(index).wait_send()

    for step in range(3):
        @pl.loop(0, chunks)
        def _(chunk):
            for copy in halo_copies(step, chunk):
                copy.wait_send()


def is_paired(bundles, width):
    return bundles == 2 and width % 128 == 0


def dot(a, b, dims=(((1,), (0,)), ((), ()))):
    return lax.dot_general(a, b, dims, precision=HIGHEST, preferred_element_type=F32)


def upper_part(value, lower=False):
    row = lax.broadcasted_iota(jnp.int32, value.shape, 0)
    col = lax.broadcasted_iota(jnp.int32, value.shape, 1)
    return jnp.where((col <= row) if lower else (col >= row), value, 0.0)


def factor_steps(block, lines, found):
    size = block.shape[0]
    if size > PANEL:
        half = size // 2
        part = []
        yield from factor_steps(block[:half, :half], lines, part)
        upper0, inverse0 = part
        corner = dot(inverse0, block[:half, half:])
        rest = block[half:, half:] - dot(corner, corner, OVER_ROWS)
        part = []
        yield from factor_steps(rest, lines, part)
        upper1, inverse1 = part
        side = -dot(inverse1, dot(corner, inverse0, OVER_ROWS))
        zero = jnp.zeros((half, size - half), F32)
        found.append(
            jnp.concatenate(
                [
                    jnp.concatenate([upper0, corner], axis=1),
                    jnp.concatenate([zero.T, upper1], axis=1),
                ],
                axis=0,
            )
        )
        found.append(
            jnp.concatenate(
                [
                    jnp.concatenate([inverse0, zero], axis=1),
                    jnp.concatenate([side, inverse1], axis=1),
                ],
                axis=0,
            )
        )
        return
    row = lax.broadcasted_iota(jnp.int32, (size, size), 0)
    col = lax.broadcasted_iota(jnp.int32, (size, size), 1)
    work = jnp.concatenate([block, (row == col).astype(F32)], axis=1)
    for first in range(0, size, GROUP):
        top = first // 8 * 8
        if first and first % 8 == 0:
            work = work[8:]
        index = lax.broadcasted_iota(jnp.int32, work.shape, 0)
        columns = [
            jnp.broadcast_to(work[:, first + j:first + j + 1], work.shape) for j in range(GROUP)
        ]
        for j in range(GROUP):
            at = first + j - top
            pivot = columns[j][at:at + 1]
            turned = 1.0 / pivot
            line = work[at:at + 1]
            lines[first + j:first + j + 1] = line * lax.rsqrt(pivot)
            factor = jnp.where(index > at, columns[j], 0.0)
            for m in range(j + 1, GROUP):
                columns[m] = columns[m] - factor * (columns[m][at:at + 1] * turned)
            work = work - factor * (line * turned)
        if (first + GROUP) % 32 == 0 and first + GROUP < size:
            yield
    found.append(upper_part(lines[:, :size]))
    found.append(upper_part(lines[:, size:], lower=True))
    yield


def write_basis(solver, fields, basis_ref, first):
    h, l = split(solver)
    fh, fl = split(fields)
    product = lambda a, b: lax.dot_general(a, b, OVER_LAST, preferred_element_type=F32)
    basis_ref[first:first + solver.shape[0]] = product(h, fh) + (product(h, fl) + product(l, fh))


def factor_kernel(gram_ref, stacked_ref, basis_ref, factor_ref, lines):
    found = []
    for _ in factor_steps(gram_ref[...], lines, found):
        pass
    factor_ref[...] = found[0]
    bundles, share, bs, width = stacked_ref.shape
    held = [stacked_ref[b].reshape(share * bs, width) for b in range(bundles)]
    write_basis(found[1], jnp.concatenate(held, axis=1), basis_ref, 0)


def finish_kernel(corner_ref, diag_ref, cross_ref, stacked_ref, basis_ref, factor_ref, lines):
    bundles, share, bs, width = stacked_ref.shape
    upper0, inverse0 = corner_ref[0], corner_ref[1]
    field0 = stacked_ref[0].reshape(share * bs, width)
    field1 = stacked_ref[1].reshape(share * bs, width)
    corner = dot(inverse0, cross_ref[...])
    rest = diag_ref[1] - dot(corner, corner, OVER_ROWS)
    side = dot(corner, inverse0, OVER_ROWS)
    factor_ref[:width, :width] = upper0
    factor_ref[:width, width:] = corner
    factor_ref[width:, :width] = jnp.zeros((width, width), F32)
    write_basis(inverse0, field0, basis_ref, 0)
    found = []
    for _ in factor_steps(rest, lines, found):
        pass
    upper1, inverse1 = found
    factor_ref[width:, width:] = upper1
    solver = jnp.concatenate([-dot(inverse1, side), inverse1], axis=1)
    write_basis(solver, jnp.concatenate([field0, field1], axis=1), basis_ref, width)


def solution(mesh):
    rows, bundles = mesh.shape["row"], mesh.shape["bundle"]
    row_bits, bundle_bits = rows.bit_length() - 1, bundles.bit_length() - 1
    vmem = pl.BlockSpec(memory_space=pltpu.VMEM)
    smem = pl.BlockSpec(memory_space=pltpu.SMEM)

    def local(vectors, blocks, columns, bounds):
        br, bs, wide = blocks.shape
        width = vectors.shape[0]
        count = width * bundles
        share = br // bundles
        paired = is_paired(bundles, width)
        panel = min(PANEL, width) if paired else min(PANEL, count)
        block = jax.ShapeDtypeStruct((width, width), F32)
        two = jax.ShapeDtypeStruct((2, width, width), F32)
        stack = jax.ShapeDtypeStruct((bundles, share, bs, width), F32)
        if paired:
            shapes = (stack, two, two, block)
            side, sums, copies = width, 2 * row_bits + bundle_bits + 1, 3
        else:
            shapes = (stack, jax.ShapeDtypeStruct((count, count), F32))
            side, sums, copies = count, row_bits + bundle_bits, max(bundles - 1, 1)
        parts = pl.pallas_call(
            functools.partial(filter_kernel, rows, bundles, len(shapes)),
            out_shape=shapes,
            in_specs=[smem, smem, vmem, vmem],
            out_specs=tuple(vmem for _ in shapes),
            scratch_shapes=[
                pltpu.VMEM((br, 2 * bs, wide), BF16),
                pltpu.VMEM((2, 3 * br, bs, width), BF16),
                pltpu.VMEM((2, 3 * br, bs, width), BF16),
                pltpu.VMEM((4, br, bs, width), F32),
                pltpu.VMEM((3, 2, br, bs, width), F32),
                pltpu.VMEM((2 * sums + 1, side, side), F32),
                pltpu.VMEM((panel, 2 * panel), F32),
                pltpu.SemaphoreType.DMA((3, 2, 4)),
                pltpu.SemaphoreType.DMA((3, 2, 4)),
                pltpu.SemaphoreType.DMA((copies,)),
                pltpu.SemaphoreType.DMA((copies,)),
                pltpu.SemaphoreType.DMA((sums,)),
                pltpu.SemaphoreType.DMA((sums,)),
            ],
            compiler_params=pltpu.CompilerParams(
                collective_id=0, has_side_effects=True, vmem_limit_bytes=VMEM_LIMIT
            ),
        )(columns, bounds, vectors, blocks)
        operands = parts[1:] + parts[:1]
        return pl.pallas_call(
            finish_kernel if paired else factor_kernel,
            out_shape=(
                jax.ShapeDtypeStruct((count, share * bs), F32),
                jax.ShapeDtypeStruct((count, count), F32),
            ),
            in_specs=[vmem] * len(operands),
            out_specs=(vmem, vmem),
            scratch_shapes=[pltpu.VMEM((panel, 2 * panel), F32)],
            compiler_params=pltpu.CompilerParams(vmem_limit_bytes=VMEM_LIMIT),
        )(*operands)

    placed = (P("bundle", "row"), P("row", None, None), P("row", None), P())
    return jax.shard_map(
        local,
        mesh=mesh,
        in_specs=placed,
        out_specs=(P(None, ("row", "bundle")), P()),
        check_vma=False,
    )
```

time: 166 us -> 133 us (0.80)
  Pallas kernels: 164 us -> 131 us
    pallas_call x2, Pallas kernels: 164 us -> 131 us  [the longest x1 122 us: local(): pl.pallas_call(functools.partial(filter_kernel, rows, bundles, len(shapes...]
where the time goes in v2:
time: 133 us
  Pallas kernels  131 us (98%)
  local copies, waits for them, and re-layouts  1.37 us (1%)
    pallas_call x1, Pallas kernels, local(): pl.pallas_call(functools.partial(filter_kernel, rows, bundles, len(shapes...  122 us
    pallas_call x1, Pallas kernels, local(): pl.pallas_call(finish_kernel if paired else factor_kernel, out_shape=(jax...  8.79 us

profile of v2, /device:TPU:0, one launch (start us, length us, event | category | flops | bytes accessed | tf_op | source)
XLA Modules:
  0.0 133.1 jit_solution(18410463126940072793)
XLA Ops:
  0.6 1.4 %copy.6.cols_ref = s32[32,6]{1,0:T(8,128)} copy(s32[32,6]{0,1:T(8,128)} %param.6) | data formatting | bytes 1536 | tf_op args[2]
  2.0 122.3 %shard_map.59 = (f32[2,16,64,128]{3,2,1,0:T(8,128)}, f32[2,128,128]{2,1,0:T(8,128)}, f32[2,128,128]{2,1,0:T(8,128)}, f32[128,128]{1,0:T(8,128)}) custom-call(s32[32,6]{1,0:T(8,128)} %copy.6.cols_ref, f32[2]{0:T(128)} %bounds_ref.1, f32[128,2048]{1,0:T(8,128)} %vec_ref.1, f32[32,64,384]{2,1,0:T(8,128)} %blocks_ref.1), custom_call_target="tpu_custom_call" | custom-call | tf_op jit(solution)/shard_map/pallas_call | solution.py:415
  124.3 8.8 %shard_map.60 = (f32[256,1024]{1,0:T(8,128)}, f32[256,256]{1,0:T(8,128)}) custom-call(f32[2,128,128]{2,1,0:T(8,128)} %get-tuple-element.6.corner_ref, f32[2,128,128]{2,1,0:T(8,128)} %get-tuple-element.7.diag_ref, f32[128,128]{1,0:T(8,128)} %get-tuple-element.8.cross_ref, f32[2,16,64,128]{3,2,1,0:T(8,128)} %get-tuple-element.9.stacked_ref), custom_call_target="tpu_custom_call" | custom-call | tf_op jit(solution)/shard_map/pallas_call | solution.py:440

commit v3 on v2

--- a/solution.py
+++ b/solution.py
@@ -14,6 +14,7 @@
 VMEM_LIMIT = 56 * 1024 * 1024
 PANEL = 64
 GROUP = 4
+CHUNKS = 4
 OVER_ROWS = (((0,), (0,)), ((), ()))
 OVER_LAST = (((1,), (1,)), ((), ()))
 
@@ -24,13 +25,10 @@
 
 
 def filter_kernel(
-    rows, bundles, out_count, cols_ref, bounds_ref, vec_ref, blocks_ref, *refs,
+    rows, bundles, cols_ref, bounds_ref, vec_ref, blocks_ref, stacked_ref, gram_ref,
+    ablk, high, low, fields, halo, sums, halo_send, halo_recv, all_send, all_recv,
+    sum_send, sum_recv,
 ):
-    outs = refs[:out_count]
-    (
-        ablk, high, low, fields, halo, sums, lines, halo_send, halo_recv, all_send, all_recv,
-        sum_send, sum_recv,
-    ) = refs[out_count:]
     me = lax.axis_index("row")
     mine = lax.axis_index("bundle")
     br, bs = blocks_ref.shape[0], blocks_ref.shape[1]
@@ -164,121 +162,280 @@
             device_id_type=MESH,
         )
 
+    def sum_step(index, device):
+        copy = sum_copy(index, device)
+        copy.start()
+        copy.wait()
+        sums[2 * index + 2] = sums[2 * index] + sums[2 * index + 1]
+
+    @pl.loop(0, chunks)
+    def _(chunk):
+        apply_chunk(2, chunk)
+
+    def stack_copy(index):
+        target = others[index]
+        return pltpu.make_async_remote_copy(
+            src_ref=fields.at[3, pl.ds(target["bundle"] * share, share)],
+            dst_ref=stacked_ref.at[mine],
+            send_sem=all_send.at[index],
+            recv_sem=all_recv.at[index],
+            device_id=target,
+            device_id_type=MESH,
+        )
+
+    for index in range(bundles - 1):
+        stack_copy(index).start()
+    stacked_ref[mine] = fields[3, pl.ds(mine * share, share)]
+    for index in range(bundles - 1):
+        stack_copy(index).wait_recv()
+    held = [stacked_ref[b].reshape(share * bs, width) for b in range(bundles)]
+    h, l = split(jnp.concatenate(held, axis=1))
+    main = lax.dot_general(h, h, OVER_ROWS, preferred_element_type=F32)
+    cross = lax.dot_general(h, l, OVER_ROWS, preferred_element_type=F32)
+    sums[0] = main + (cross + cross.T)
+    for index, device in enumerate(partners):
+        sum_step(index, device)
+    gram_ref[...] = sums[2 * len(partners)]
+    for index in range(bundles - 1):
+        stack_copy(index).wait_send()
+
+    for step in range(3):
+        @pl.loop(0, chunks)
+        def _(chunk):
+            for copy in halo_copies(step, chunk):
+                copy.wait_send()
+
+
+def paired_kernel(
+    rows, cols_ref, bounds_ref, vec_ref, blocks_ref, stacked_ref, corner_ref, diag_ref, cross_ref,
+    ablk, picks, fields, halo, whole, arrived, sums, lines, halo_send, halo_recv, all_send,
+    all_recv, sum_send, sum_recv,
+):
+    me = lax.axis_index("row")
+    mine = lax.axis_index("bundle")
+    theirs = 1 - mine
+    br, bs = blocks_ref.shape[0], blocks_ref.shape[1]
+    slots = cols_ref.shape[1]
+    width = vec_ref.shape[0]
+    part = width // 2
+    total = br * rows
+    pairs = br // 2
+    chunks = CHUNKS
+    per = pairs // chunks
+    right = lax.rem(me + 1, rows)
+    left = lax.rem(me + rows - 1, rows)
+    row_bits = rows.bit_length() - 1
+    partners = []
+    for bit in range(row_bits):
+        mask = 1 << bit
+        upper = lax.rem(lax.div(me, mask), 2)
+        partners.append({"row": me + mask - 2 * mask * upper})
+    partners.append({"bundle": theirs})
+
+    barrier = pltpu.get_barrier_semaphore()
+    greeted = [{"row": left}, {"row": right}] + partners
+    for device in greeted:
+        pl.semaphore_signal(barrier, inc=1, device_id=device, device_id_type=MESH)
+
+    center = (bounds_ref[0] + bounds_ref[1]) * 0.5
+    inverse = 1.0 / ((bounds_ref[1] - bounds_ref[0]) * 0.5)
+    in_low = lax.broadcasted_iota(jnp.int32, (bs, width), 1) < part
+    turn = lambda value: pltpu.roll(value, part, 1)
+
+    def halo_copies(step, half, chunk):
+        span = pl.ds(chunk * per, per)
+        return [
+            pltpu.make_async_remote_copy(
+                src_ref=fields.at[half, step, span],
+                dst_ref=halo.at[step, half, side, span],
+                send_sem=halo_send.at[step, half, side, chunk],
+                recv_sem=halo_recv.at[step, half, side, chunk],
+                device_id={"row": target},
+                device_id_type=MESH,
+            )
+            for side, target in ((0, right), (1, left))
+        ]
+
+    def keep(half, pair, value):
+        h = value.astype(BF16).astype(F32)
+        l = value - h
+        picks[half, 2 * pair] = jnp.where(in_low, h, turn(l)).astype(BF16)
+        picks[half, 2 * pair + 1] = jnp.where(in_low, turn(h), l).astype(BF16)
+
+    def unpack(even_half, odd_half):
+        return (
+            jnp.where(in_low, even_half, turn(odd_half)),
+            jnp.where(in_low, turn(even_half), odd_half),
+        )
+
+    for pair in range(pairs):
+        turned = vec_ref[:, pair * 2 * bs:(pair + 1) * 2 * bs].T
+        fields[0, 0, pair], fields[1, 0, pair] = unpack(turned[:bs], turned[bs:])
+        if pair == per - 1:
+            pl.semaphore_wait(barrier, len(greeted))
+        if (pair + 1) % per == 0:
+            for copy in halo_copies(0, 0, pair // per):
+                copy.start()
+
+    @pl.loop(0, chunks)
+    def _(chunk):
+        for copy in halo_copies(0, 1, chunk):
+            copy.start()
+
+    @pl.loop(0, br)
+    def _(i):
+        h, l = split(blocks_ref[i])
+        ablk[i, :bs] = h
+        ablk[i, bs:] = l
+
+    def receive(step, half):
+        @pl.loop(0, pairs, unroll=2)
+        def _(pair):
+            keep(half, pairs + pair, fields[half, step, pair])
+
+        @pl.loop(0, chunks)
+        def _(chunk):
+            for side, copy in enumerate(halo_copies(step, half, chunk)):
+                copy.wait_recv()
+                for inner in range(per):
+                    pair = chunk * per + inner
+                    keep(half, side * 2 * pairs + pair, halo[step, half, side, pair])
+
+    def apply_chunk(step, half, chunk):
+        @pl.loop(0, per, unroll=per)
+        def _(inner):
+            pair = chunk * per + inner
+            results = []
+            for odd in range(2):
+                i = 2 * pair + odd
+                found = []
+                for s in range(slots):
+                    c = cols_ref[i, s] - me * br + br
+                    c = jnp.where(c < 0, c + total, c)
+                    c = jnp.where(c >= total, c - total, c)
+                    found.append(picks[half, jnp.clip(c, 0, 3 * br - 1)])
+                out = jnp.dot(ablk[i], jnp.concatenate(found, axis=0), preferred_element_type=F32)
+                result = out[:bs] + out[bs:]
+                results.append(result + turn(result))
+            result = jnp.where(in_low, results[0], results[1])
+            value = (result - center * fields[half, step, pair]) * inverse
+            if step > 0:
+                value = 2.0 * value - fields[half, step - 1, pair]
+            fields[half, step + 1, pair] = value
+
+    for step in range(2):
+        for half in range(2):
+            receive(step, half)
+
+            @pl.loop(0, chunks)
+            def _(chunk):
+                apply_chunk(step, half, chunk)
+                for copy in halo_copies(step + 1, half, chunk):
+                    copy.start()
+
+    share = pairs // 2
+    parts = chunks // 2
+
+    def stack_copy(half, index):
+        return pltpu.make_async_remote_copy(
+            src_ref=fields.at[half, 3, pl.ds(theirs * share + index * per, per)],
+            dst_ref=arrived.at[half, pl.ds(index * per, per)],
+            send_sem=all_send.at[half, index],
+            recv_sem=all_recv.at[half, index],
+            device_id={"bundle": theirs},
+            device_id_type=MESH,
+        )
+
+    for half in range(2):
+        receive(2, half)
+
+        @pl.loop(0, parts)
+        def _(index):
+            apply_chunk(2, half, theirs * parts + index)
+            stack_copy(half, index).start()
+
+        @pl.loop(0, parts)
+        def _(index):
+            apply_chunk(2, half, mine * parts + index)
+
+    @pl.loop(0, pairs, unroll=2)
+    def _(pair):
+        whole[2 * pair], whole[2 * pair + 1] = unpack(fields[0, 3, pair], fields[1, 3, pair])
+
+    stacked_ref[mine] = whole[pl.ds(mine * 2 * share, 2 * share)]
+    h, l = split(whole[...].reshape(br * bs, width))
+    both = lax.dot_general(
+        h, jnp.concatenate([h, l], axis=1), OVER_ROWS, preferred_element_type=F32
+    )
+    sums[0] = both[:, :width] + (both[:, width:] + both[:, width:].T)
+
     def sum_step(index, device, beside=None):
-        copy = sum_copy(index, device)
+        copy = pltpu.make_async_remote_copy(
+            src_ref=sums.at[2 * index],
+            dst_ref=sums.at[2 * index + 1],
+            send_sem=sum_send.at[index],
+            recv_sem=sum_recv.at[index],
+            device_id=device,
+            device_id_type=MESH,
+        )
         copy.start()
         if beside is not None:
             next(beside, None)
         copy.wait()
         sums[2 * index + 2] = sums[2 * index] + sums[2 * index + 1]
 
-    if is_paired(bundles, width):
-        stacked_ref, corner_ref, diag_ref, cross_ref = outs
-        theirs = 1 - mine
-        half = chunks // 2
-
-        def stack_copy(part):
-            rows_of = pl.ds(theirs * share + part * per, per)
-            return pltpu.make_async_remote_copy(
-                src_ref=fields.at[3, rows_of],
-                dst_ref=stacked_ref.at[mine, pl.ds(part * per, per)],
-                send_sem=all_send.at[part],
-                recv_sem=all_recv.at[part],
-                device_id={"bundle": theirs},
-                device_id_type=MESH,
-            )
-
-        @pl.loop(0, half)
-        def _(part):
-            apply_chunk(2, theirs * half + part)
-            stack_copy(part).start()
-
-        @pl.loop(0, half)
-        def _(part):
-            apply_chunk(2, mine * half + part)
-
-        stacked_ref[mine] = fields[3, pl.ds(mine * share, share)]
-        h, l = split(fields[3].reshape(br * bs, width))
-        both = lax.dot_general(
-            h, jnp.concatenate([h, l], axis=1), OVER_ROWS, preferred_element_type=F32
-        )
-        sums[0] = both[:, :width] + (both[:, width:] + both[:, width:].T)
-        for index in range(row_bits):
-            sum_step(index, partners[index])
-        done = 2 * row_bits
-        diag_ref[mine] = sums[done]
-        diag_copy = pltpu.make_async_remote_copy(
-            src_ref=sums.at[done],
-            dst_ref=diag_ref.at[mine],
-            send_sem=all_send.at[half],
-            recv_sem=all_recv.at[half],
-            device_id={"bundle": theirs},
-            device_id_type=MESH,
-        )
-        diag_copy.start()
-        for part in range(half):
-            stack_copy(part).wait_recv()
-        h0, l0 = split(stacked_ref[0].reshape(share * bs, width))
-        h1, l1 = split(stacked_ref[1].reshape(share * bs, width))
-        both = lax.dot_general(
-            h0, jnp.concatenate([h1, l1], axis=1), OVER_ROWS, preferred_element_type=F32
-        )
-        rest = lax.dot_general(l0, h1, OVER_ROWS, preferred_element_type=F32)
-        sums[done + 2] = both[:, :width] + (both[:, width:] + rest)
-        diag_copy.wait()
-        found = []
-        pieces = factor_steps(diag_ref[0], lines, found)
-        for bit, device in enumerate(partners):
-            sum_step(row_bits + 1 + bit, device, pieces)
-        for _ in pieces:
-            pass
-        cross_ref[...] = sums[done + 2 + 2 * len(partners)]
-        corner_ref[0], corner_ref[1] = found
-        for part in range(half):
-            stack_copy(part).wait_send()
-    else:
-        stacked_ref, gram_ref = outs
-
-        @pl.loop(0, chunks)
-        def _(chunk):
-            apply_chunk(2, chunk)
-
-        def stack_copy(index):
-            target = others[index]
-            return pltpu.make_async_remote_copy(
-                src_ref=fields.at[3, pl.ds(target["bundle"] * share, share)],
-                dst_ref=stacked_ref.at[mine],
-                send_sem=all_send.at[index],
-                recv_sem=all_recv.at[index],
-                device_id=target,
-                device_id_type=MESH,
-            )
-
-        for index in range(bundles - 1):
-            stack_copy(index).start()
-        stacked_ref[mine] = fields[3, pl.ds(mine * share, share)]
-        for index in range(bundles - 1):
-            stack_copy(index).wait_recv()
-        held = [stacked_ref[b].reshape(share * bs, width) for b in range(bundles)]
-        h, l = split(jnp.concatenate(held, axis=1))
-        main = lax.dot_general(h, h, OVER_ROWS, preferred_element_type=F32)
-        cross = lax.dot_general(h, l, OVER_ROWS, preferred_element_type=F32)
-        sums[0] = main + (cross + cross.T)
-        for index, device in enumerate(partners):
-            sum_step(index, device)
-        gram_ref[...] = sums[2 * len(partners)]
-        for index in range(bundles - 1):
-            stack_copy(index).wait_send()
-
-    for step in range(3):
-        @pl.loop(0, chunks)
-        def _(chunk):
-            for copy in halo_copies(step, chunk):
-                copy.wait_send()
+    for index in range(row_bits):
+        sum_step(index, partners[index])
+    done = 2 * row_bits
+    diag_ref[mine] = sums[done]
+    diag_copy = pltpu.make_async_remote_copy(
+        src_ref=sums.at[done],
+        dst_ref=diag_ref.at[mine],
+        send_sem=sum_send.at[row_bits],
+        recv_sem=sum_recv.at[row_bits],
+        device_id={"bundle": theirs},
+        device_id_type=MESH,
+    )
+    diag_copy.start()
+    for half in range(2):
+        for index in range(parts):
+            stack_copy(half, index).wait_recv()
+
+    @pl.loop(0, share, unroll=2)
+    def _(pair):
+        even, odd = unpack(arrived[0, pair], arrived[1, pair])
+        stacked_ref[theirs, 2 * pair] = even
+        stacked_ref[theirs, 2 * pair + 1] = odd
+
+    h0, l0 = split(stacked_ref[0].reshape(2 * share * bs, width))
+    h1, l1 = split(stacked_ref[1].reshape(2 * share * bs, width))
+    both = lax.dot_general(
+        h0, jnp.concatenate([h1, l1], axis=1), OVER_ROWS, preferred_element_type=F32
+    )
+    rest = lax.dot_general(l0, h1, OVER_ROWS, preferred_element_type=F32)
+    sums[done + 2] = both[:, :width] + (both[:, width:] + rest)
+    diag_copy.wait()
+    found = []
+    pieces = factor_steps(diag_ref[0], lines, found)
+    for bit, device in enumerate(partners):
+        sum_step(row_bits + 1 + bit, device, pieces)
+    for _ in pieces:
+        pass
+    cross_ref[...] = sums[done + 2 + 2 * len(partners)]
+    corner_ref[0], corner_ref[1] = found
+
+    for half in range(2):
+        for index in range(parts):
+            stack_copy(half, index).wait_send()
+        for step in range(3):
+            @pl.loop(0, chunks)
+            def _(chunk):
+                for copy in halo_copies(step, half, chunk):
+                    copy.wait_send()
 
 
 def is_paired(bundles, width):
-    return bundles == 2 and width % 128 == 0
+    return bundles == 2 and width == 128
 
 
 def dot(a, b, dims=(((1,), (0,)), ((), ()))):
@@ -406,32 +563,51 @@
         block = jax.ShapeDtypeStruct((width, width), F32)
         two = jax.ShapeDtypeStruct((2, width, width), F32)
         stack = jax.ShapeDtypeStruct((bundles, share, bs, width), F32)
+        dma = pltpu.SemaphoreType.DMA
         if paired:
+            sums = 2 * row_bits + 2
+            kernel = functools.partial(paired_kernel, rows)
             shapes = (stack, two, two, block)
-            side, sums, copies = width, 2 * row_bits + bundle_bits + 1, 3
+            scratch = [
+                pltpu.VMEM((br, 2 * bs, wide), BF16),
+                pltpu.VMEM((2, 3 * br, bs, width), BF16),
+                pltpu.VMEM((2, 4, br // 2, bs, width), F32),
+                pltpu.VMEM((3, 2, 2, br // 2, bs, width), F32),
+                pltpu.VMEM((br, bs, width), F32),
+                pltpu.VMEM((2, br // 4, bs, width), F32),
+                pltpu.VMEM((2 * sums + 1, width, width), F32),
+                pltpu.VMEM((panel, 2 * panel), F32),
+                dma((3, 2, 2, CHUNKS)),
+                dma((3, 2, 2, CHUNKS)),
+                dma((2, CHUNKS // 2)),
+                dma((2, CHUNKS // 2)),
+                dma((sums,)),
+                dma((sums,)),
+            ]
         else:
+            sums = row_bits + bundle_bits
+            kernel = functools.partial(filter_kernel, rows, bundles)
             shapes = (stack, jax.ShapeDtypeStruct((count, count), F32))
-            side, sums, copies = count, row_bits + bundle_bits, max(bundles - 1, 1)
-        parts = pl.pallas_call(
-            functools.partial(filter_kernel, rows, bundles, len(shapes)),
-            out_shape=shapes,
-            in_specs=[smem, smem, vmem, vmem],
-            out_specs=tuple(vmem for _ in shapes),
-            scratch_shapes=[
+            scratch = [
                 pltpu.VMEM((br, 2 * bs, wide), BF16),
                 pltpu.VMEM((2, 3 * br, bs, width), BF16),
                 pltpu.VMEM((2, 3 * br, bs, width), BF16),
                 pltpu.VMEM((4, br, bs, width), F32),
                 pltpu.VMEM((3, 2, br, bs, width), F32),
-                pltpu.VMEM((2 * sums + 1, side, side), F32),
-                pltpu.VMEM((panel, 2 * panel), F32),
-                pltpu.SemaphoreType.DMA((3, 2, 4)),
-                pltpu.SemaphoreType.DMA((3, 2, 4)),
-                pltpu.SemaphoreType.DMA((copies,)),
-                pltpu.SemaphoreType.DMA((copies,)),
-                pltpu.SemaphoreType.DMA((sums,)),
-                pltpu.SemaphoreType.DMA((sums,)),
-            ],
+                pltpu.VMEM((2 * sums + 1, count, count), F32),
+                dma((3, 2, 4)),
+                dma((3, 2, 4)),
+                dma((max(bundles - 1, 1),)),
+                dma((max(bundles - 1, 1),)),
+                dma((sums,)),
+                dma((sums,)),
+            ]
+        parts = pl.pallas_call(
+            kernel,
+            out_shape=shapes,
+            in_specs=[smem, smem, vmem, vmem],
+            out_specs=tuple(vmem for _ in shapes),
+            scratch_shapes=scratch,
             compiler_params=pltpu.CompilerParams(
                 collective_id=0, has_side_effects=True, vmem_limit_bytes=VMEM_LIMIT
             ),

time: 133 us -> 125 us (0.940)
  Pallas kernels: 131 us -> 122 us
    pallas_call x1, Pallas kernels: 122 us -> 114 us  [local(): pl.pallas_call(kernel, out_shape=shapes, in_specs=[smem, smem, vmem, vmem...]
where the time goes in v3:
time: 125 us; the launch traced here: 124 us
  Pallas kernels  122 us (98%)
  local copies, waits for them, and re-layouts  1.37 us (1%)
    pallas_call x1, Pallas kernels, local(): pl.pallas_call(kernel, out_shape=shapes, in_specs=[smem, smem, vmem, vmem...  114 us
    pallas_call x1, Pallas kernels, local(): pl.pallas_call(finish_kernel if paired else factor_kernel, out_shape=(jax...  8.79 us

profile of v3, /device:TPU:0, one launch (start us, length us, event | category | flops | bytes accessed | tf_op | source)
XLA Modules:
  0.0 124.3 jit_solution(11637812421781222507)
XLA Ops:
  0.6 1.4 %copy.6.cols_ref = s32[32,6]{1,0:T(8,128)} copy(s32[32,6]{0,1:T(8,128)} %param.6) | data formatting | bytes 1536 | tf_op args[2]
  2.0 113.5 %shard_map.59 = (f32[2,16,64,128]{3,2,1,0:T(8,128)}, f32[2,128,128]{2,1,0:T(8,128)}, f32[2,128,128]{2,1,0:T(8,128)}, f32[128,128]{1,0:T(8,128)}) custom-call(s32[32,6]{1,0:T(8,128)} %copy.6.cols_ref, f32[2]{0:T(128)} %bounds_ref.1, f32[128,2048]{1,0:T(8,128)} %vec_ref.1, f32[32,64,384]{2,1,0:T(8,128)} %blocks_ref.1), custom_call_target="tpu_custom_call" | custom-call | tf_op jit(solution)/shard_map/pallas_call | solution.py:605
  115.5 8.8 %shard_map.60 = (f32[256,1024]{1,0:T(8,128)}, f32[256,256]{1,0:T(8,128)}) custom-call(f32[2,128,128]{2,1,0:T(8,128)} %get-tuple-element.6.corner_ref, f32[2,128,128]{2,1,0:T(8,128)} %get-tuple-element.7.diag_ref, f32[128,128]{1,0:T(8,128)} %get-tuple-element.8.cross_ref, f32[2,16,64,128]{3,2,1,0:T(8,128)} %get-tuple-element.9.stacked_ref), custom_call_target="tpu_custom_call" | custom-call | tf_op jit(solution)/shard_map/pallas_call | solution.py:616

commit v4 on v3

--- a/solution.py
+++ b/solution.py
@@ -13,7 +13,7 @@
 HIGHEST = lax.Precision.HIGHEST
 VMEM_LIMIT = 56 * 1024 * 1024
 PANEL = 64
-GROUP = 4
+GROUP = 8
 CHUNKS = 4
 OVER_ROWS = (((0,), (0,)), ((), ()))
 OVER_LAST = (((1,), (1,)), ((), ()))
@@ -207,15 +207,15 @@
 
 
 def paired_kernel(
-    rows, cols_ref, bounds_ref, vec_ref, blocks_ref, stacked_ref, corner_ref, diag_ref, cross_ref,
-    ablk, picks, fields, halo, whole, arrived, sums, lines, halo_send, halo_recv, all_send,
+    rows, cols_in, bounds_ref, vec_in, blocks_in, stacked_ref, corner_ref, diag_ref, cross_ref,
+    cols_ref, vec_ref, blocks_ref, load_sem, ablk, picks, fields, halo, whole, arrived, sums, lines, halo_send, halo_recv, all_send,
     all_recv, sum_send, sum_recv,
 ):
     me = lax.axis_index("row")
     mine = lax.axis_index("bundle")
     theirs = 1 - mine
     br, bs = blocks_ref.shape[0], blocks_ref.shape[1]
-    slots = cols_ref.shape[1]
+    slots = cols_ref.shape[0]
     width = vec_ref.shape[0]
     part = width // 2
     total = br * rows
@@ -237,6 +237,15 @@
     for device in greeted:
         pl.semaphore_signal(barrier, inc=1, device_id=device, device_id_type=MESH)
 
+    loads = [
+        pltpu.make_async_copy(source, target, load_sem.at[index])
+        for index, (source, target) in enumerate(
+            ((vec_in, vec_ref), (blocks_in, blocks_ref), (cols_in, cols_ref))
+        )
+    ]
+    for load in loads:
+        load.start()
+
     center = (bounds_ref[0] + bounds_ref[1]) * 0.5
     inverse = 1.0 / ((bounds_ref[1] - bounds_ref[0]) * 0.5)
     in_low = lax.broadcasted_iota(jnp.int32, (bs, width), 1) < part
@@ -268,6 +277,7 @@
             jnp.where(in_low, turn(even_half), odd_half),
         )
 
+    loads[0].wait()
     for pair in range(pairs):
         turned = vec_ref[:, pair * 2 * bs:(pair + 1) * 2 * bs].T
         fields[0, 0, pair], fields[1, 0, pair] = unpack(turned[:bs], turned[bs:])
@@ -281,6 +291,9 @@
     def _(chunk):
         for copy in halo_copies(0, 1, chunk):
             copy.start()
+
+    loads[1].wait()
+    loads[2].wait()
 
     @pl.loop(0, br)
     def _(i):
@@ -310,7 +323,7 @@
                 i = 2 * pair + odd
                 found = []
                 for s in range(slots):
-                    c = cols_ref[i, s] - me * br + br
+                    c = cols_ref[s, i] - me * br + br
                     c = jnp.where(c < 0, c + total, c)
                     c = jnp.where(c >= total, c - total, c)
                     found.append(picks[half, jnp.clip(c, 0, 3 * br - 1)])
@@ -552,6 +565,7 @@
     row_bits, bundle_bits = rows.bit_length() - 1, bundles.bit_length() - 1
     vmem = pl.BlockSpec(memory_space=pltpu.VMEM)
     smem = pl.BlockSpec(memory_space=pltpu.SMEM)
+    hbm = pl.BlockSpec(memory_space=pl.ANY)
 
     def local(vectors, blocks, columns, bounds):
         br, bs, wide = blocks.shape
@@ -569,6 +583,10 @@
             kernel = functools.partial(paired_kernel, rows)
             shapes = (stack, two, two, block)
             scratch = [
+                pltpu.SMEM(columns.shape[::-1], jnp.int32),
+                pltpu.VMEM(vectors.shape, F32),
+                pltpu.VMEM(blocks.shape, F32),
+                dma((3,)),
                 pltpu.VMEM((br, 2 * bs, wide), BF16),
                 pltpu.VMEM((2, 3 * br, bs, width), BF16),
                 pltpu.VMEM((2, 4, br // 2, bs, width), F32),
@@ -605,13 +623,13 @@
         parts = pl.pallas_call(
             kernel,
             out_shape=shapes,
-            in_specs=[smem, smem, vmem, vmem],
+            in_specs=[hbm, smem, hbm, hbm] if paired else [smem, smem, vmem, vmem],
             out_specs=tuple(vmem for _ in shapes),
             scratch_shapes=scratch,
             compiler_params=pltpu.CompilerParams(
                 collective_id=0, has_side_effects=True, vmem_limit_bytes=VMEM_LIMIT
             ),
-        )(columns, bounds, vectors, blocks)
+        )(columns.T if paired else columns, bounds, vectors, blocks)
         operands = parts[1:] + parts[:1]
         return pl.pallas_call(
             finish_kernel if paired else factor_kernel,

time: 125 us -> 120 us (0.960)
  Pallas kernels: 122 us -> 120 us
  local copies, waits for them, and re-layouts: 1.37 us -> 0 us
    pallas_call x1, Pallas kernels: 114 us -> 112 us  [local(): pl.pallas_call(kernel, out_shape=shapes, in_specs=[hbm, smem, hbm, hbm] i...]
    unnamed x1 -> x0, local copies, waits for them, and re-layouts: 1.37 us -> none
where the time goes in v4:
time: 120 us
  Pallas kernels  120 us (100%)
    pallas_call x1, Pallas kernels, local(): pl.pallas_call(kernel, out_shape=shapes, in_specs=[hbm, smem, hbm, hbm] i...  112 us
    pallas_call x1, Pallas kernels, local(): pl.pallas_call(finish_kernel if paired else factor_kernel, out_shape=(jax...  7.59 us

profile of v4, /device:TPU:0, one launch (start us, length us, event | category | flops | bytes accessed | tf_op | source)
XLA Modules:
  0.0 120.2 jit_solution(16841095388364709249)
XLA Ops:
  0.6 112.0 %shard_map.59 = (f32[2,16,64,128]{3,2,1,0:T(8,128)}, f32[2,128,128]{2,1,0:T(8,128)}, f32[2,128,128]{2,1,0:T(8,128)}, f32[128,128]{1,0:T(8,128)}) custom-call(s32[6,32]{1,0:T(8,128)} %bitcast.1, f32[2]{0:T(128)} %bounds_ref.1, f32[128,2048]{1,0:T(8,128)} %vec_in.1, f32[32,64,384]{2,1,0:T(8,128)} %blocks_in.1), custom_call_target="tpu_custom_call" | custom-call | tf_op jit(solution)/shard_map/pallas_call | solution.py:623
  112.6 7.6 %shard_map.60 = (f32[256,1024]{1,0:T(8,128)}, f32[256,256]{1,0:T(8,128)}) custom-call(f32[2,128,128]{2,1,0:T(8,128)} %get-tuple-element.6.corner_ref, f32[2,128,128]{2,1,0:T(8,128)} %get-tuple-element.7.diag_ref, f32[128,128]{1,0:T(8,128)} %get-tuple-element.8.cross_ref, f32[2,16,64,128]{3,2,1,0:T(8,128)} %get-tuple-element.9.stacked_ref), custom_call_target="tpu_custom_call" | custom-call | tf_op jit(solution)/shard_map/pallas_call | solution.py:634
